TPU v7x, 512 devices: a whole 4x4x16 slice. The times are simulated.
512 devices in a mesh: net: 64 (over z, x), scen: 8 (over y, core).
Axes of the slice: x: 4, y: 4, z: 16, core: 2. Of those that a mesh axis runs over, the one named last changes fastest.
Arguments:
- device_group: int32 [64], replicated, may hold values from 3 to 63, as said below
- column_blocks: int32 [256, 12], P('net'), may hold values from 0 to 255, as said below
- impedance_real: bfloat16 [256, 12, 128, 128], P('net'), may hold values from 0 to 0.015258789
- impedance_imag: bfloat16 [256, 12, 128, 128], P('net'), may hold values from 0 to 0.0076293945
- building_phase: int32 [65536], P('net'), may hold values from 0 to 32767, as said below
- building_power: float32 [65536], P('net'), may hold values from 0.2 to 1
- reactive_ratio: float32 [65536], P('net'), may hold values from 0.1 to 0.8
- copula_normals: float32 [65536, 1024], P('net', 'scen'), may hold values from -6 to 6
- source_angle: float32 [32768], P('net'), may hold values from -3.140625 to 3.140625
Outputs:
- voltage_real: float32 [32768, 1024], P('net', 'scen')
- voltage_imag: float32 [32768, 1024], P('net', 'scen')
- drop_mean: float32 [32768, 16], P('net')
Inputs may be any that keep to these rules, and one draw needn't show every extreme that they name: `device_group`: never falling along the devices; each group is a run of 1 to 4 consecutive devices and is labelled by the index of its last device; the first 4 devices form one group. `column_blocks`: slot 0 of block row r is r itself; the first min(12, 4 times the devices of r's group) slots are distinct blocks of devices of r's group; the other slots repeat r. `building_phase`: building b feeds a phase of the device that holds b: from 512 * (b // 1024) to that plus 512 - 1; every phase is fed by at least one building.
All inputs are finite; a program needn't handle non-finite values.
Results may differ from a plain program's by a relative error of at most 0.0063.
Values may be sent and summed in bfloat16 or wider, within the bound.
No kernel may reach another device: no remote copies, remote signals or barrier semaphores. Data moves between devices by JAX's collectives and lax.ppermute only.
A program may use at most 64 MiB of HBM per device.

v0:
```python
import jax
import jax.numpy as jnp
from jax import lax
from jax.sharding import PartitionSpec as P

GMAX = 4
ITERS = 3
TIMES = 16


floor_square = 0.49


def from_behind(value, axis, steps):
    count = lax.axis_size(axis)
    leading, last = (max(0, -steps), min(count, count - steps))
    return lax.ppermute(value, axis, [(source, source + steps) for source in range(leading, last)])


def shards(
    device_group,
    column_blocks,
    impedance_real,
    impedance_imag,
    building_phase,
    building_power,
    reactive_ratio,
    copula_normals,
    source_angle,
):
    block_count, slot_count, block_width, other_width = impedance_real.shape
    phase_count = block_count * block_width
    column_count = copula_normals.shape[1]
    local_scen = column_count // TIMES
    total_scen = local_scen * lax.axis_size("scen")
    scenario = (
        lax.axis_index("scen") * local_scen + jnp.arange(column_count, dtype=jnp.int32) // TIMES
    ).astype(jnp.float32)
    scen_level = 0.5 + scenario / (total_scen - 1)
    real_power = (
        building_power[:, None] * scen_level[None, :] * jnp.exp(0.4 * copula_normals - 0.08)
    )
    both_power = jnp.concatenate([real_power, real_power * reactive_ratio[:, None]], axis=1)
    net_index = lax.axis_index("net")
    local_phase = building_phase - net_index * phase_count
    loads = jax.ops.segment_sum(both_power, local_phase, num_segments=phase_count)
    load_real = loads[:, :column_count]
    load_reactive = loads[:, column_count:]
    source_real = jnp.broadcast_to(jnp.cos(source_angle)[:, None], (phase_count, column_count))
    source_imag = jnp.broadcast_to(jnp.sin(source_angle)[:, None], (phase_count, column_count))
    own_group = device_group[net_index]
    group_size = jnp.sum((device_group == own_group).astype(jnp.int32))
    live_count = jnp.minimum(slot_count, group_size * block_count)
    live_slots = jnp.arange(slot_count, dtype=jnp.int32) < live_count
    owner_device = column_blocks // block_count
    window_index = (
        owner_device - net_index + (GMAX - 1)
    ) * block_count + column_blocks % block_count
    volt_real = source_real
    volt_imag = source_imag
    for sweep in range(ITERS):
        mag_square = jnp.maximum(volt_real * volt_real + volt_imag * volt_imag, floor_square)
        current_real = (load_real * volt_real + load_reactive * volt_imag) / mag_square
        current_imag = (load_real * volt_imag - load_reactive * volt_real) / mag_square
        currents = jnp.concatenate([current_real, current_imag], axis=1).astype(jnp.bfloat16)
        lower_parts = []
        upper_parts = []
        for distance in range(1, GMAX):
            lower_parts.append(from_behind(currents, "net", distance))
            upper_parts.append(from_behind(currents, "net", -distance))
        nearby = jnp.concatenate(lower_parts[::-1] + [currents] + upper_parts, axis=0).reshape(
            -1, block_width, 2 * column_count
        )
        gathered = jnp.take(nearby, window_index, axis=0)
        gathered = jnp.where(live_slots[None, :, None, None], gathered, jnp.zeros((), jnp.bfloat16))
        real_part = jnp.einsum(
            "bsij,bsjk->bik", impedance_real, gathered, preferred_element_type=jnp.float32
        ).reshape(phase_count, 2 * column_count)
        imag_part = jnp.einsum(
            "bsij,bsjk->bik", impedance_imag, gathered, preferred_element_type=jnp.float32
        ).reshape(phase_count, 2 * column_count)
        drop_real = real_part[:, :column_count] - imag_part[:, column_count:]
        drop_imag = real_part[:, column_count:] + imag_part[:, :column_count]
        volt_real = source_real - drop_real
        volt_imag = source_imag - drop_imag
    magnitude = jnp.sqrt(volt_real * volt_real + volt_imag * volt_imag)
    local_sum = jnp.sum(magnitude.reshape(phase_count, local_scen, TIMES), axis=1)
    scen_total = lax.psum(local_sum, "scen")
    drop_mean = 100.0 * (1.0 - scen_total / total_scen)
    return (volt_real, volt_imag, drop_mean)


def solution(mesh):
    in_specs = (
        P(),
        P("net", None),
        P("net", None, None, None),
        P("net", None, None, None),
        P("net"),
        P("net"),
        P("net"),
        P("net", "scen"),
        P("net"),
    )
    out_specs = (P("net", "scen"), P("net", "scen"), P("net", None))
    return jax.shard_map(shards, mesh=mesh, in_specs=in_specs, out_specs=out_specs, check_vma=False)
```

profile of v0, /device:TPU:224, one launch (start us, length us, event | category | flops | bytes accessed | tf_op | source)
XLA Modules:
  0.0 170.0 jit_solution(13973513056029608391)
XLA Ops:
  0.7 0.8 fusion.42
  2.2 1.4 broadcast_multiply_fusion
  3.6 6.2 %scatter_custom_fusion = f32[512,256]{1,0:T(8,128)S(1)} fusion(s32[1024]{0:T(1024)S(1)} %broadcast_subtract_fusion, f32[1024,128]{1,0:T(8,128)S(1)} %get-tuple-element.12, f32[]{:T(128)} %constant.112, f32[1024,128]{1,0:T(8,128)S(1)} %get-tuple-element.13, f32[]{:T(128)} %constant.78.clone.1), kind=kCustom, calls=%fused_computation.7 | custom fusion | flops 524288 | bytes 1572872 | tf_op jit(solution)/shard_map/scatter-add | solution.py:46
  10.2 4.7 %collective-permute-start = (bf16[512,256]{1,0:T(8,128)(2,1)S(1)}, bf16[512,256]{1,0:T(8,128)(2,1)}, u32[]{:S(2)}, u32[]{:S(2)}) collective-permute-start(bf16[512,256]{1,0:T(8,128)(2,1)S(1)} %pad_maximum_fusion), channel_id=1, source_target_pairs={{0,24},{8,32},{16,40},{24,48},{32,56},{40,64},{48,72},{56,80},{64,... | collective-permute-start | bytes 786440 | tf_op jit(solution)/shard_map/ppermute | solution.py:17
  14.9 5.3 %collective-permute-start.1 = (bf16[512,256]{1,0:T(8,128)(2,1)S(1)}, bf16[512,256]{1,0:T(8,128)(2,1)}, u32[]{:S(2)}, u32[]{:S(2)}) collective-permute-start(bf16[512,256]{1,0:T(8,128)(2,1)S(1)} %pad_maximum_fusion), channel_id=1, source_target_pairs={{0,16},{8,24},{16,32},{24,40},{32,48},{40,56},{48,64},{56,72},{64,... | collective-permute-start | bytes 786440 | tf_op jit(solution)/shard_map/ppermute | solution.py:17
  20.1 2.8 %collective-permute-start.2 = (bf16[512,256]{1,0:T(8,128)(2,1)S(1)}, bf16[512,256]{1,0:T(8,128)(2,1)S(1)}, u32[]{:S(2)}, u32[]{:S(2)}) collective-permute-start(bf16[512,256]{1,0:T(8,128)(2,1)S(1)} %pad_maximum_fusion), channel_id=1, source_target_pairs={{0,8},{8,16},{16,24},{24,32},{32,40},{40,48},{48,56},{56,64},{64,7... | collective-permute-start | bytes 786440 | tf_op jit(solution)/shard_map/ppermute | solution.py:17
  22.9 5.2 %collective-permute-start.3 = (bf16[512,256]{1,0:T(8,128)(2,1)S(1)}, bf16[512,256]{1,0:T(8,128)(2,1)S(1)}, u32[]{:S(2)}, u32[]{:S(2)}) collective-permute-start(bf16[512,256]{1,0:T(8,128)(2,1)S(1)} %pad_maximum_fusion), channel_id=1, source_target_pairs={{8,0},{16,8},{24,16},{32,24},{40,32},{48,40},{56,48},{64,56},{72,6... | collective-permute-start | bytes 786440 | tf_op jit(solution)/shard_map/ppermute | solution.py:17
  28.1 1.9 %collective-permute-start.4 = (bf16[512,256]{1,0:T(8,128)(2,1)S(1)}, bf16[512,256]{1,0:T(8,128)(2,1)S(1)}, u32[]{:S(2)}, u32[]{:S(2)}) collective-permute-start(bf16[512,256]{1,0:T(8,128)(2,1)S(1)} %pad_maximum_fusion), channel_id=1, source_target_pairs={{16,0},{24,8},{32,16},{40,24},{48,32},{56,40},{64,48},{72,56},{80,... | collective-permute-start | bytes 786440 | tf_op jit(solution)/shard_map/ppermute | solution.py:17
  30.7 1.3 fusion.27
  32.7 1.9 %collective-permute-start.5 = (bf16[512,256]{1,0:T(8,128)(2,1)S(1)}, bf16[512,256]{1,0:T(8,128)(2,1)S(1)}, u32[]{:S(2)}, u32[]{:S(2)}) collective-permute-start(bf16[512,256]{1,0:T(8,128)(2,1)S(1)} %pad_maximum_fusion), channel_id=1, source_target_pairs={{24,0},{32,8},{40,16},{48,24},{56,32},{64,40},{72,48},{80,56},{88,... | collective-permute-start | bytes 786440 | tf_op jit(solution)/shard_map/ppermute | solution.py:17
  34.6 1.7 constant_dynamic-update-slice_fusion.6
  36.3 1.7 constant_dynamic-update-slice_fusion.5
  38.7 0.7 constant_dynamic-update-slice_fusion.3
  39.4 0.7 constant_dynamic-update-slice_fusion.2
  40.2 5.0 %collective-permute-done.4 = bf16[512,256]{1,0:T(8,128)(2,1)S(1)} collective-permute-done((bf16[512,256]{1,0:T(8,128)(2,1)S(1)}, bf16[512,256]{1,0:T(8,128)(2,1)S(1)}, u32[]{:S(2)}, u32[]{:S(2)}) %collective-permute-start.4) | collective-permute-done | bytes 262176 | tf_op jit(solution)/shard_map/ppermute | solution.py:17
  45.2 0.7 constant_dynamic-update-slice_fusion.1
  45.9 0.7 constant_dynamic-update-slice_fusion
  46.7 4.0 %gather_fusion = bf16[48,128,256]{2,1,0:T(8,128)(2,1)} fusion(bf16[28,128,256]{2,1,0:T(8,128)(2,1)} %bitcast.1, s32[1024]{0:T(1024)S(1)} %pad_clamp_fusion), kind=kCustom, calls=%fused_computation.clone | custom fusion | bytes 6291648 | tf_op jit(solution)/shard_map/jit(_take)/gather | solution.py:74
  50.7 2.8 %fusion.4 = f32[4,256,128,1]{1,2,3,0:T(8,128)S(1)} fusion(bf16[4,12,128,128]{3,2,1,0:T(8,128)(2,1)S(1)} %copy-done, bf16[4,12,128,256]{3,2,1,0:T(8,128)(2,1)} %bitcast.53, pred[12]{0:T(512)(128)(4,1)S(1)} %iota_compare_fusion, pred[4,12]{1,0:T(4,128)(4,1)S(1)} %get-tuple-element.10), kind=kOutput, calls=%fused_computation.11 | convolution fusion | flops 405798912 | bytes 5242940 | tf_op jit(solution)/shard_map/bsij,bsjk->bik/dot_general | solution.py:76
  54.0 0.8 fusion.5
  55.0 1.9 %collective-permute-start.6 = (bf16[512,256]{1,0:T(8,128)(2,1)S(1)}, bf16[512,256]{1,0:T(8,128)(2,1)S(1)}, u32[]{:S(2)}, u32[]{:S(2)}) collective-permute-start(bf16[512,256]{1,0:T(8,128)(2,1)S(1)} %pad_maximum_fusion.1), channel_id=1, source_target_pairs={{0,24},{8,32},{16,40},{24,48},{32,56},{40,64},{48,72},{56,80},{64,... | collective-permute-start | bytes 786440 | tf_op jit(solution)/shard_map/ppermute | solution.py:17
  57.0 10.6 %collective-permute-start.7 = (bf16[512,256]{1,0:T(8,128)(2,1)S(1)}, bf16[512,256]{1,0:T(8,128)(2,1)S(1)}, u32[]{:S(2)}, u32[]{:S(2)}) collective-permute-start(bf16[512,256]{1,0:T(8,128)(2,1)S(1)} %pad_maximum_fusion.1), channel_id=1, source_target_pairs={{0,16},{8,24},{16,32},{24,40},{32,48},{40,56},{48,64},{56,72},{64,... | collective-permute-start | bytes 786440 | tf_op jit(solution)/shard_map/ppermute | solution.py:17
  67.6 1.9 %collective-permute-start.8 = (bf16[512,256]{1,0:T(8,128)(2,1)S(1)}, bf16[512,256]{1,0:T(8,128)(2,1)S(1)}, u32[]{:S(2)}, u32[]{:S(2)}) collective-permute-start(bf16[512,256]{1,0:T(8,128)(2,1)S(1)} %pad_maximum_fusion.1), channel_id=1, source_target_pairs={{0,8},{8,16},{16,24},{24,32},{32,40},{40,48},{48,56},{56,64},{64,7... | collective-permute-start | bytes 786440 | tf_op jit(solution)/shard_map/ppermute | solution.py:17
  69.5 6.0 %collective-permute-start.9 = (bf16[512,256]{1,0:T(8,128)(2,1)S(1)}, bf16[512,256]{1,0:T(8,128)(2,1)S(1)}, u32[]{:S(2)}, u32[]{:S(2)}) collective-permute-start(bf16[512,256]{1,0:T(8,128)(2,1)S(1)} %pad_maximum_fusion.1), channel_id=1, source_target_pairs={{8,0},{16,8},{24,16},{32,24},{40,32},{48,40},{56,48},{64,56},{72,6... | collective-permute-start | bytes 786440 | tf_op jit(solution)/shard_map/ppermute | solution.py:17
  75.5 1.9 %collective-permute-start.10 = (bf16[512,256]{1,0:T(8,128)(2,1)S(1)}, bf16[512,256]{1,0:T(8,128)(2,1)S(1)}, u32[]{:S(2)}, u32[]{:S(2)}) collective-permute-start(bf16[512,256]{1,0:T(8,128)(2,1)S(1)} %pad_maximum_fusion.1), channel_id=1, source_target_pairs={{16,0},{24,8},{32,16},{40,24},{48,32},{56,40},{64,48},{72,56},{80,... | collective-permute-start | bytes 786440 | tf_op jit(solution)/shard_map/ppermute | solution.py:17
  77.5 1.9 %collective-permute-start.11 = (bf16[512,256]{1,0:T(8,128)(2,1)S(1)}, bf16[512,256]{1,0:T(8,128)(2,1)S(1)}, u32[]{:S(2)}, u32[]{:S(2)}) collective-permute-start(bf16[512,256]{1,0:T(8,128)(2,1)S(1)} %pad_maximum_fusion.1), channel_id=1, source_target_pairs={{24,0},{32,8},{40,16},{48,24},{56,32},{64,40},{72,48},{80,56},{88,... | collective-permute-start | bytes 786440 | tf_op jit(solution)/shard_map/ppermute | solution.py:17
  81.6 0.7 constant_dynamic-update-slice_fusion.10
  82.3 0.7 constant_dynamic-update-slice_fusion.9
  83.1 7.1 %collective-permute-done.10 = bf16[512,256]{1,0:T(8,128)(2,1)S(1)} collective-permute-done((bf16[512,256]{1,0:T(8,128)(2,1)S(1)}, bf16[512,256]{1,0:T(8,128)(2,1)S(1)}, u32[]{:S(2)}, u32[]{:S(2)}) %collective-permute-start.10) | collective-permute-done | bytes 262176 | tf_op jit(solution)/shard_map/ppermute | solution.py:17
  90.2 0.7 constant_dynamic-update-slice_fusion.8
  90.9 0.7 constant_dynamic-update-slice_fusion.7
  91.7 4.0 %gather_fusion.1 = bf16[48,128,256]{2,1,0:T(8,128)(2,1)} fusion(bf16[28,128,256]{2,1,0:T(8,128)(2,1)} %bitcast.15, s32[1024]{0:T(1024)S(1)} %pad_clamp_fusion), kind=kCustom, calls=%fused_computation.1.clone | custom fusion | bytes 6291648 | tf_op jit(solution)/shard_map/jit(_take)/gather | solution.py:74
  95.7 2.8 %fusion.6 = f32[4,256,128,1]{1,2,3,0:T(8,128)S(1)} fusion(bf16[4,12,128,128]{3,2,1,0:T(8,128)(2,1)S(1)} %copy-done, bf16[4,12,128,256]{3,2,1,0:T(8,128)(2,1)} %bitcast.55, pred[12]{0:T(512)(128)(4,1)S(1)} %iota_compare_fusion, pred[4,12]{1,0:T(4,128)(4,1)S(1)} %get-tuple-element.10), kind=kOutput, calls=%fused_computation.13 | convolution fusion | flops 405798912 | bytes 5242940 | tf_op jit(solution)/shard_map/bsij,bsjk->bik/dot_general | solution.py:76
  99.0 0.8 fusion.7
  100.1 1.9 %collective-permute-start.12 = (bf16[512,256]{1,0:T(8,128)(2,1)S(1)}, bf16[512,256]{1,0:T(8,128)(2,1)S(1)}, u32[]{:S(2)}, u32[]{:S(2)}) collective-permute-start(bf16[512,256]{1,0:T(8,128)(2,1)S(1)} %pad_maximum_fusion.2), channel_id=1, source_target_pairs={{0,24},{8,32},{16,40},{24,48},{32,56},{40,64},{48,72},{56,80},{64,... | collective-permute-start | bytes 786440 | tf_op jit(solution)/shard_map/ppermute | solution.py:17
  102.0 5.8 %collective-permute-start.13 = (bf16[512,256]{1,0:T(8,128)(2,1)S(1)}, bf16[512,256]{1,0:T(8,128)(2,1)S(1)}, u32[]{:S(2)}, u32[]{:S(2)}) collective-permute-start(bf16[512,256]{1,0:T(8,128)(2,1)S(1)} %pad_maximum_fusion.2), channel_id=1, source_target_pairs={{0,16},{8,24},{16,32},{24,40},{32,48},{40,56},{48,64},{56,72},{64,... | collective-permute-start | bytes 786440 | tf_op jit(solution)/shard_map/ppermute | solution.py:17
  107.8 3.5 %collective-permute-start.14 = (bf16[512,256]{1,0:T(8,128)(2,1)S(1)}, bf16[512,256]{1,0:T(8,128)(2,1)S(1)}, u32[]{:S(2)}, u32[]{:S(2)}) collective-permute-start(bf16[512,256]{1,0:T(8,128)(2,1)S(1)} %pad_maximum_fusion.2), channel_id=1, source_target_pairs={{0,8},{8,16},{16,24},{24,32},{32,40},{40,48},{48,56},{56,64},{64,7... | collective-permute-start | bytes 786440 | tf_op jit(solution)/shard_map/ppermute | solution.py:17
  111.3 5.5 %collective-permute-start.15 = (bf16[512,256]{1,0:T(8,128)(2,1)S(1)}, bf16[512,256]{1,0:T(8,128)(2,1)S(1)}, u32[]{:S(2)}, u32[]{:S(2)}) collective-permute-start(bf16[512,256]{1,0:T(8,128)(2,1)S(1)} %pad_maximum_fusion.2), channel_id=1, source_target_pairs={{8,0},{16,8},{24,16},{32,24},{40,32},{48,40},{56,48},{64,56},{72,6... | collective-permute-start | bytes 786440 | tf_op jit(solution)/shard_map/ppermute | solution.py:17
  116.8 3.4 %collective-permute-start.16 = (bf16[512,256]{1,0:T(8,128)(2,1)S(1)}, bf16[512,256]{1,0:T(8,128)(2,1)S(1)}, u32[]{:S(2)}, u32[]{:S(2)}) collective-permute-start(bf16[512,256]{1,0:T(8,128)(2,1)S(1)} %pad_maximum_fusion.2), channel_id=1, source_target_pairs={{16,0},{24,8},{32,16},{40,24},{48,32},{56,40},{64,48},{72,56},{80,... | collective-permute-start | bytes 786440 | tf_op jit(solution)/shard_map/ppermute | solution.py:17
  120.2 1.9 %collective-permute-start.17 = (bf16[512,256]{1,0:T(8,128)(2,1)S(1)}, bf16[512,256]{1,0:T(8,128)(2,1)S(1)}, u32[]{:S(2)}, u32[]{:S(2)}) collective-permute-start(bf16[512,256]{1,0:T(8,128)(2,1)S(1)} %pad_maximum_fusion.2), channel_id=1, source_target_pairs={{24,0},{32,8},{40,16},{48,24},{56,32},{64,40},{72,48},{80,56},{88,... | collective-permute-start | bytes 786440 | tf_op jit(solution)/shard_map/ppermute | solution.py:17
  122.2 4.5 %collective-permute-done.14 = bf16[512,256]{1,0:T(8,128)(2,1)S(1)} collective-permute-done((bf16[512,256]{1,0:T(8,128)(2,1)S(1)}, bf16[512,256]{1,0:T(8,128)(2,1)S(1)}, u32[]{:S(2)}, u32[]{:S(2)}) %collective-permute-start.14) | collective-permute-done | bytes 262176 | tf_op jit(solution)/shard_map/ppermute | solution.py:17
  126.7 7.5 %collective-permute-done.16 = bf16[512,256]{1,0:T(8,128)(2,1)S(1)} collective-permute-done((bf16[512,256]{1,0:T(8,128)(2,1)S(1)}, bf16[512,256]{1,0:T(8,128)(2,1)S(1)}, u32[]{:S(2)}, u32[]{:S(2)}) %collective-permute-start.16) | collective-permute-done | bytes 262176 | tf_op jit(solution)/shard_map/ppermute | solution.py:17
  134.2 1.5 collective-permute-done.17
  135.8 2.5 %gather_fusion.2 = bf16[48,128,256]{2,1,0:T(8,128)(2,1)} fusion(bf16[28,128,256]{2,1,0:T(8,128)(2,1)S(1)} %bitcast.50, s32[1024]{0:T(1024)S(1)} %pad_clamp_fusion), kind=kCustom, calls=%fused_computation.2.clone | custom fusion | bytes 6291648 | tf_op jit(solution)/shard_map/jit(_take)/gather | solution.py:74
  138.3 2.8 %fusion.8 = f32[4,256,128,1]{1,2,3,0:T(8,128)S(1)} fusion(bf16[4,12,128,128]{3,2,1,0:T(8,128)(2,1)S(1)} %copy-done, bf16[4,12,128,256]{3,2,1,0:T(8,128)(2,1)} %bitcast.51, pred[12]{0:T(512)(128)(4,1)S(1)} %iota_compare_fusion, pred[4,12]{1,0:T(4,128)(4,1)S(1)} %get-tuple-element.10), kind=kOutput, calls=%fused_computation.15 | convolution fusion | flops 405798912 | bytes 5242940 | tf_op jit(solution)/shard_map/bsij,bsjk->bik/dot_general | solution.py:76
  141.6 0.8 fusion.9
  142.4 1.0 add_sqrt_fusion
  143.6 25.8 %psum.7 = f32[512,16]{0,1:T(8,128)S(1)} all-reduce(f32[512,16]{0,1:T(8,128)S(1)} %reduce_sum.19), channel_id=1, replica_groups=mesh['net'=64,'scen'=8] {'scen'}, use_global_device_ids=true, to_apply=%region_3.5 | all-reduce | flops 8192 | bytes 65536 | tf_op jit(solution)/shard_map/psum | solution.py:88
  (59 shorter events, 7.4 us)
Async XLA Ops:
  0.6 50.0 %copy-start = (bf16[4,12,128,128]{3,2,1,0:T(8,128)(2,1)S(1)}, bf16[4,12,128,128]{3,2,1,0:T(8,128)(2,1)}, u32[]{:S(2)}) copy-start(bf16[4,12,128,128]{3,2,1,0:T(8,128)(2,1)} %param.13) | copy-start | bytes 4718596
  3.6 26.5 %copy-start.4 = (s32[4,12]{1,0:T(4,128)S(1)}, s32[4,12]{1,0:T(4,128)}, u32[]{:S(2)}) copy-start(s32[4,12]{1,0:T(4,128)} %param.12) | copy-start | bytes 580
  3.6 26.6 %copy-start.8 = (s32[64]{0:T(128)S(1)}, s32[64]{0:T(128)}, u32[]{:S(2)}) copy-start(s32[64]{0:T(128)} %param.11) | copy-start | bytes 772
  10.2 22.5 %collective-permute-start = (bf16[512,256]{1,0:T(8,128)(2,1)S(1)}, bf16[512,256]{1,0:T(8,128)(2,1)}, u32[]{:S(2)}, u32[]{:S(2)}) collective-permute-start(bf16[512,256]{1,0:T(8,128)(2,1)S(1)} %pad_maximum_fusion), channel_id=1, source_target_pairs={{0,24},{8,32},{16,40},{24,48},{32,56},{40,64},{48,72},{56,80},{64,... | collective-permute-start | bytes 786440 | tf_op jit(solution)/shard_map/ppermute | solution.py:17
  14.9 21.4 %collective-permute-start.1 = (bf16[512,256]{1,0:T(8,128)(2,1)S(1)}, bf16[512,256]{1,0:T(8,128)(2,1)}, u32[]{:S(2)}, u32[]{:S(2)}) collective-permute-start(bf16[512,256]{1,0:T(8,128)(2,1)S(1)} %pad_maximum_fusion), channel_id=1, source_target_pairs={{0,16},{8,24},{16,32},{24,40},{32,48},{40,56},{48,64},{56,72},{64,... | collective-permute-start | bytes 786440 | tf_op jit(solution)/shard_map/ppermute | solution.py:17
  20.1 17.8 %collective-permute-start.2 = (bf16[512,256]{1,0:T(8,128)(2,1)S(1)}, bf16[512,256]{1,0:T(8,128)(2,1)S(1)}, u32[]{:S(2)}, u32[]{:S(2)}) collective-permute-start(bf16[512,256]{1,0:T(8,128)(2,1)S(1)} %pad_maximum_fusion), channel_id=1, source_target_pairs={{0,8},{8,16},{16,24},{24,32},{32,40},{40,48},{48,56},{56,64},{64,7... | collective-permute-start | bytes 786440 | tf_op jit(solution)/shard_map/ppermute | solution.py:17
  22.9 16.5 %collective-permute-start.3 = (bf16[512,256]{1,0:T(8,128)(2,1)S(1)}, bf16[512,256]{1,0:T(8,128)(2,1)S(1)}, u32[]{:S(2)}, u32[]{:S(2)}) collective-permute-start(bf16[512,256]{1,0:T(8,128)(2,1)S(1)} %pad_maximum_fusion), channel_id=1, source_target_pairs={{8,0},{16,8},{24,16},{32,24},{40,32},{48,40},{56,48},{64,56},{72,6... | collective-permute-start | bytes 786440 | tf_op jit(solution)/shard_map/ppermute | solution.py:17
  28.1 17.1 %collective-permute-start.4 = (bf16[512,256]{1,0:T(8,128)(2,1)S(1)}, bf16[512,256]{1,0:T(8,128)(2,1)S(1)}, u32[]{:S(2)}, u32[]{:S(2)}) collective-permute-start(bf16[512,256]{1,0:T(8,128)(2,1)S(1)} %pad_maximum_fusion), channel_id=1, source_target_pairs={{16,0},{24,8},{32,16},{40,24},{48,32},{56,40},{64,48},{72,56},{80,... | collective-permute-start | bytes 786440 | tf_op jit(solution)/shard_map/ppermute | solution.py:17
  32.7 13.2 %collective-permute-start.5 = (bf16[512,256]{1,0:T(8,128)(2,1)S(1)}, bf16[512,256]{1,0:T(8,128)(2,1)S(1)}, u32[]{:S(2)}, u32[]{:S(2)}) collective-permute-start(bf16[512,256]{1,0:T(8,128)(2,1)S(1)} %pad_maximum_fusion), channel_id=1, source_target_pairs={{24,0},{32,8},{40,16},{48,24},{56,32},{64,40},{72,48},{80,56},{88,... | collective-permute-start | bytes 786440 | tf_op jit(solution)/shard_map/ppermute | solution.py:17
  50.7 2.9 %copy-start.2 = (bf16[48,128,256]{2,1,0:T(8,128)(2,1)S(1)}, bf16[48,128,256]{2,1,0:T(8,128)(2,1)}, u32[]{:S(2)}) copy-start(bf16[48,128,256]{2,1,0:T(8,128)(2,1)} %gather_fusion) | copy-start | bytes 9437188
  50.7 3.3 %copy-start.5 = (bf16[4,12,128,128]{3,2,1,0:T(8,128)(2,1)S(1)}, bf16[4,12,128,128]{3,2,1,0:T(8,128)(2,1)}, u32[]{:S(2)}) copy-start(bf16[4,12,128,128]{3,2,1,0:T(8,128)(2,1)} %param.14) | copy-start | bytes 4718596
  55.0 22.4 %collective-permute-start.6 = (bf16[512,256]{1,0:T(8,128)(2,1)S(1)}, bf16[512,256]{1,0:T(8,128)(2,1)S(1)}, u32[]{:S(2)}, u32[]{:S(2)}) collective-permute-start(bf16[512,256]{1,0:T(8,128)(2,1)S(1)} %pad_maximum_fusion.1), channel_id=1, source_target_pairs={{0,24},{8,32},{16,40},{24,48},{32,56},{40,64},{48,72},{56,80},{64,... | collective-permute-start | bytes 786440 | tf_op jit(solution)/shard_map/ppermute | solution.py:17
  57.0 23.1 %collective-permute-start.7 = (bf16[512,256]{1,0:T(8,128)(2,1)S(1)}, bf16[512,256]{1,0:T(8,128)(2,1)S(1)}, u32[]{:S(2)}, u32[]{:S(2)}) collective-permute-start(bf16[512,256]{1,0:T(8,128)(2,1)S(1)} %pad_maximum_fusion.1), channel_id=1, source_target_pairs={{0,16},{8,24},{16,32},{24,40},{32,48},{40,56},{48,64},{56,72},{64,... | collective-permute-start | bytes 786440 | tf_op jit(solution)/shard_map/ppermute | solution.py:17
  67.6 13.3 %collective-permute-start.8 = (bf16[512,256]{1,0:T(8,128)(2,1)S(1)}, bf16[512,256]{1,0:T(8,128)(2,1)S(1)}, u32[]{:S(2)}, u32[]{:S(2)}) collective-permute-start(bf16[512,256]{1,0:T(8,128)(2,1)S(1)} %pad_maximum_fusion.1), channel_id=1, source_target_pairs={{0,8},{8,16},{16,24},{24,32},{32,40},{40,48},{48,56},{56,64},{64,7... | collective-permute-start | bytes 786440 | tf_op jit(solution)/shard_map/ppermute | solution.py:17
  69.5 12.8 %collective-permute-start.9 = (bf16[512,256]{1,0:T(8,128)(2,1)S(1)}, bf16[512,256]{1,0:T(8,128)(2,1)S(1)}, u32[]{:S(2)}, u32[]{:S(2)}) collective-permute-start(bf16[512,256]{1,0:T(8,128)(2,1)S(1)} %pad_maximum_fusion.1), channel_id=1, source_target_pairs={{8,0},{16,8},{24,16},{32,24},{40,32},{48,40},{56,48},{64,56},{72,6... | collective-permute-start | bytes 786440 | tf_op jit(solution)/shard_map/ppermute | solution.py:17
  75.5 14.6 %collective-permute-start.10 = (bf16[512,256]{1,0:T(8,128)(2,1)S(1)}, bf16[512,256]{1,0:T(8,128)(2,1)S(1)}, u32[]{:S(2)}, u32[]{:S(2)}) collective-permute-start(bf16[512,256]{1,0:T(8,128)(2,1)S(1)} %pad_maximum_fusion.1), channel_id=1, source_target_pairs={{16,0},{24,8},{32,16},{40,24},{48,32},{56,40},{64,48},{72,56},{80,... | collective-permute-start | bytes 786440 | tf_op jit(solution)/shard_map/ppermute | solution.py:17
  77.5 13.5 %collective-permute-start.11 = (bf16[512,256]{1,0:T(8,128)(2,1)S(1)}, bf16[512,256]{1,0:T(8,128)(2,1)S(1)}, u32[]{:S(2)}, u32[]{:S(2)}) collective-permute-start(bf16[512,256]{1,0:T(8,128)(2,1)S(1)} %pad_maximum_fusion.1), channel_id=1, source_target_pairs={{24,0},{32,8},{40,16},{48,24},{56,32},{64,40},{72,48},{80,56},{88,... | collective-permute-start | bytes 786440 | tf_op jit(solution)/shard_map/ppermute | solution.py:17
  95.7 2.9 %copy-start.3 = (bf16[48,128,256]{2,1,0:T(8,128)(2,1)S(1)}, bf16[48,128,256]{2,1,0:T(8,128)(2,1)}, u32[]{:S(2)}) copy-start(bf16[48,128,256]{2,1,0:T(8,128)(2,1)} %gather_fusion.1) | copy-start | bytes 9437188
  95.7 3.3 %copy-start.6 = (bf16[4,12,128,128]{3,2,1,0:T(8,128)(2,1)S(1)}, bf16[4,12,128,128]{3,2,1,0:T(8,128)(2,1)}, u32[]{:S(2)}) copy-start(bf16[4,12,128,128]{3,2,1,0:T(8,128)(2,1)} %param.14) | copy-start | bytes 4718596
  100.1 20.1 %collective-permute-start.12 = (bf16[512,256]{1,0:T(8,128)(2,1)S(1)}, bf16[512,256]{1,0:T(8,128)(2,1)S(1)}, u32[]{:S(2)}, u32[]{:S(2)}) collective-permute-start(bf16[512,256]{1,0:T(8,128)(2,1)S(1)} %pad_maximum_fusion.2), channel_id=1, source_target_pairs={{0,24},{8,32},{16,40},{24,48},{32,56},{40,64},{48,72},{56,80},{64,... | collective-permute-start | bytes 786440 | tf_op jit(solution)/shard_map/ppermute | solution.py:17
  102.0 20.2 %collective-permute-start.13 = (bf16[512,256]{1,0:T(8,128)(2,1)S(1)}, bf16[512,256]{1,0:T(8,128)(2,1)S(1)}, u32[]{:S(2)}, u32[]{:S(2)}) collective-permute-start(bf16[512,256]{1,0:T(8,128)(2,1)S(1)} %pad_maximum_fusion.2), channel_id=1, source_target_pairs={{0,16},{8,24},{16,32},{24,40},{32,48},{40,56},{48,64},{56,72},{64,... | collective-permute-start | bytes 786440 | tf_op jit(solution)/shard_map/ppermute | solution.py:17
  107.8 18.8 %collective-permute-start.14 = (bf16[512,256]{1,0:T(8,128)(2,1)S(1)}, bf16[512,256]{1,0:T(8,128)(2,1)S(1)}, u32[]{:S(2)}, u32[]{:S(2)}) collective-permute-start(bf16[512,256]{1,0:T(8,128)(2,1)S(1)} %pad_maximum_fusion.2), channel_id=1, source_target_pairs={{0,8},{8,16},{16,24},{24,32},{32,40},{40,48},{48,56},{56,64},{64,7... | collective-permute-start | bytes 786440 | tf_op jit(solution)/shard_map/ppermute | solution.py:17
  111.3 15.4 %collective-permute-start.15 = (bf16[512,256]{1,0:T(8,128)(2,1)S(1)}, bf16[512,256]{1,0:T(8,128)(2,1)S(1)}, u32[]{:S(2)}, u32[]{:S(2)}) collective-permute-start(bf16[512,256]{1,0:T(8,128)(2,1)S(1)} %pad_maximum_fusion.2), channel_id=1, source_target_pairs={{8,0},{16,8},{24,16},{32,24},{40,32},{48,40},{56,48},{64,56},{72,6... | collective-permute-start | bytes 786440 | tf_op jit(solution)/shard_map/ppermute | solution.py:17
  116.8 17.4 %collective-permute-start.16 = (bf16[512,256]{1,0:T(8,128)(2,1)S(1)}, bf16[512,256]{1,0:T(8,128)(2,1)S(1)}, u32[]{:S(2)}, u32[]{:S(2)}) collective-permute-start(bf16[512,256]{1,0:T(8,128)(2,1)S(1)} %pad_maximum_fusion.2), channel_id=1, source_target_pairs={{16,0},{24,8},{32,16},{40,24},{48,32},{56,40},{64,48},{72,56},{80,... | collective-permute-start | bytes 786440 | tf_op jit(solution)/shard_map/ppermute | solution.py:17
  120.2 15.6 %collective-permute-start.17 = (bf16[512,256]{1,0:T(8,128)(2,1)S(1)}, bf16[512,256]{1,0:T(8,128)(2,1)S(1)}, u32[]{:S(2)}, u32[]{:S(2)}) collective-permute-start(bf16[512,256]{1,0:T(8,128)(2,1)S(1)} %pad_maximum_fusion.2), channel_id=1, source_target_pairs={{24,0},{32,8},{40,16},{48,24},{56,32},{64,40},{72,48},{80,56},{88,... | collective-permute-start | bytes 786440 | tf_op jit(solution)/shard_map/ppermute | solution.py:17
  138.3 2.9 %copy-start.1 = (bf16[48,128,256]{2,1,0:T(8,128)(2,1)S(1)}, bf16[48,128,256]{2,1,0:T(8,128)(2,1)}, u32[]{:S(2)}) copy-start(bf16[48,128,256]{2,1,0:T(8,128)(2,1)} %gather_fusion.2) | copy-start | bytes 9437188
  138.3 3.3 %copy-start.7 = (bf16[4,12,128,128]{3,2,1,0:T(8,128)(2,1)S(1)}, bf16[4,12,128,128]{3,2,1,0:T(8,128)(2,1)}, u32[]{:S(2)}) copy-start(bf16[4,12,128,128]{3,2,1,0:T(8,128)(2,1)} %param.14) | copy-start | bytes 4718596
where the time goes:
time: 171 us; the launch traced here: 170 us
  starting transfers between devices  68 us (40%)
  blocking collectives  25.8 us (15%)
  waiting for transfers between devices  25.7 us (15%)
  local copies, waits for them, and re-layouts  24.2 us (14%)
  other arithmetic  13.6 us (8%)
  matrix products  10.9 us (6%)
  between operations  1.72 us (1%)
    ppermute x18, starting transfers between devices, from_behind(): lax.ppermute(value, axis, [(source, source + steps) for source in range(l...  68 us
    psum x1, blocking collectives, shards(): scen_total = lax.psum(local_sum, 'scen')  25.8 us
    ppermute x18, waiting for transfers between devices, from_behind(): lax.ppermute(value, axis, [(source, source + steps) for source in range(l...  25.7 us
    unnamed x33, local copies, waits for them, and re-layouts  10.6 us
    gather x3, local copies, waits for them, and re-layouts, shards(): gathered = jnp.take(nearby, window_index, axis=0)  10.5 us
    dot_general x3, matrix products, shards(): jnp.einsum('bsij,bsjk->bik', impedance_real, gathered, preferred_element_...  8.52 us
    scatter-add x1, other arithmetic, shards(): jax.ops.segment_sum(both_power, local_phase, num_segments=phase_count)  6.25 us
  transfers between devices with their start and end apart: 18, of which 5 were waited for; matrix products, arithmetic and copies ran while one was open for 7% of the time, Pallas kernels for 0%

commit v1 on v0

v1 whole, which is shorter than its diff:
```python
import functools

import jax
import jax.numpy as jnp
from jax import lax
from jax.experimental import pallas as pl
from jax.experimental.pallas import tpu as pltpu
from jax.sharding import PartitionSpec as P

GMAX = 4
ITERS = 3
TIMES = 16
FLOOR = 0.49
LANES = 128
VMEM_BYTES = 24 * 1024 * 1024
f32, bf16 = jnp.float32, jnp.bfloat16


def split3(value):
    high = value.astype(bf16)
    rest = value - high.astype(f32)
    middle = rest.astype(bf16)
    return high, middle, (rest - middle.astype(f32)).astype(bf16)


def currents_of(volt_real, volt_imag, load_real, load_reactive):
    inverse = 1.0 / jnp.maximum(volt_real * volt_real + volt_imag * volt_imag, FLOOR)
    current_real = (load_real * volt_real + load_reactive * volt_imag) * inverse
    current_imag = (load_real * volt_imag - load_reactive * volt_real) * inverse
    return current_real.astype(bf16), current_imag.astype(bf16)


def front_kernel(where, group_ref, phase_ref, power_ref, ratio_ref, normals_ref, angle_ref,
                 place_ref, current_ref, load_real_ref, load_reactive_ref, source_real_ref, source_imag_ref, *, net_count, scen_total):
    net_index, scen_index = where[0], where[1]
    own = group_ref[net_index]
    before = jnp.int32(0)
    for distance in range(1, GMAX):
        other = group_ref[jnp.maximum(net_index - distance, 0)]
        before += ((net_index >= distance) & (other == own)).astype(jnp.int32)
    size = own - (net_index - before) + 1
    start = net_index - before
    place_ref[0] = jnp.where(size == 1, 0, jnp.where(size == 2, 1 + start % 2, jnp.where(size == 3, 3 + start % 3, 6 + start % 4)))
    place_ref[1] = start
    place_ref[2] = before

    blocks = phase_ref.shape[0]
    angle = angle_ref[...]
    count = angle.shape[0]
    phase_count = count * LANES
    stacked = jnp.concatenate(
        [power_ref[...], ratio_ref[...], jnp.cos(angle), jnp.sin(angle), jnp.zeros((LANES - 2 * blocks - 2 * count, LANES), f32)], axis=0)
    columns = stacked.T

    def column(k):
        return jnp.broadcast_to(columns[:, k:k + 1], (LANES, LANES))

    lane = lax.broadcasted_iota(jnp.int32, (1, LANES), 1)
    scenario = (scen_index * (LANES // TIMES) + lane // TIMES).astype(f32)
    level = 0.5 + scenario / (scen_total - 1)
    row = lax.broadcasted_iota(jnp.int32, (phase_count, LANES), 0) + net_index * phase_count
    hot, pieces = [], []
    for k in range(blocks):
        hot.append(jnp.where(row == phase_ref[k:k + 1, :], 1.0, 0.0).astype(bf16))
        part = normals_ref[k * LANES:(k + 1) * LANES, :]
        real_power = column(k) * level * jnp.exp(0.4 * part - 0.08)
        pieces.append(split3(jnp.concatenate([real_power, real_power * column(blocks + k)], axis=1)))
    hot = jnp.concatenate(hot, axis=1)
    loads = None
    for piece in zip(*pieces):
        term = jnp.dot(hot, jnp.concatenate(piece, axis=0), preferred_element_type=f32)
        loads = term if loads is None else loads + term
    load_real_ref[...] = loads[:, :LANES]
    load_reactive_ref[...] = loads[:, LANES:]
    for k in range(count):
        rows = slice(k * LANES, (k + 1) * LANES)
        source_real = column(2 * blocks + k)
        source_imag = column(2 * blocks + count + k)
        source_real_ref[rows, :] = source_real
        source_imag_ref[rows, :] = source_imag
        current_real, current_imag = currents_of(source_real, source_imag, loads[rows, :LANES], loads[rows, LANES:])
        for copy in range(GMAX):
            current_ref[copy, rows, :LANES] = current_real
            current_ref[copy, rows, LANES:] = current_imag


def front(where, group, phase, power, ratio, normals, angle, net_count, scen_total):
    building_count, columns = normals.shape
    phase_count = angle.shape[0]
    smem, vmem = pl.BlockSpec(memory_space=pltpu.SMEM), pl.BlockSpec(memory_space=pltpu.VMEM)
    return pl.pallas_call(
        functools.partial(front_kernel, net_count=net_count, scen_total=scen_total),
        out_shape=[jax.ShapeDtypeStruct((4,), jnp.int32), jax.ShapeDtypeStruct((GMAX, phase_count, 2 * columns), bf16)]
        + [jax.ShapeDtypeStruct((phase_count, columns), f32)] * 4,
        in_specs=[smem, smem] + [vmem] * 5,
        out_specs=[smem] + [vmem] * 5,
        compiler_params=pltpu.CompilerParams(vmem_limit_bytes=VMEM_BYTES),
        name="front",
    )(where, group, phase.reshape(-1, LANES), power.reshape(-1, LANES), ratio.reshape(-1, LANES), normals, angle.reshape(-1, LANES))


def sweep_kernel(place_ref, column_ref, impedance_real_ref, impedance_imag_ref, load_real_ref, load_reactive_ref,
                 source_real_ref, source_imag_ref, *refs, size, last):
    parts = 1 if size == GMAX else size
    window_refs, refs = refs[:parts], refs[parts:]
    block_count, slot_count, block_width, _ = impedance_real_ref.shape
    live = min(slot_count, size * block_count)
    if parts > 1:
        window_ref, outs = refs[-1], refs[:-1]
        for k in range(parts):
            window_ref[k * block_count:(k + 1) * block_count] = window_refs[k][...].reshape(block_count, block_width, -1)
    else:
        window_ref, outs = window_refs[0], refs
    start, before = place_ref[1], place_ref[2]
    if last:
        pick_lane = lax.broadcasted_iota(jnp.int32, (TIMES, LANES), 1)
        pick_row = lax.broadcasted_iota(jnp.int32, (TIMES, LANES), 0)
        pick = jnp.where(pick_lane % TIMES == pick_row, 1.0, 0.0).astype(bf16)
    for r in range(block_count):
        left_real, left_imag, right = [], [], []
        for s in range(live):
            member = column_ref[r, s] - start * block_count
            if size < GMAX:
                away = before - member // block_count
                away = jnp.where(away < 0, away + size, away)
                member = away * block_count + member % block_count
            left_real.append(impedance_real_ref[r, s])
            left_imag.append(impedance_imag_ref[r, s])
            right.append(window_ref[member])
        left = jnp.concatenate([jnp.concatenate(left_real, axis=1), jnp.concatenate(left_imag, axis=1)], axis=0)
        product = jnp.dot(left, jnp.concatenate(right, axis=0), preferred_element_type=f32)
        drop_real = product[:block_width, :LANES] - product[block_width:, LANES:]
        drop_imag = product[:block_width, LANES:] + product[block_width:, :LANES]
        rows = slice(r * block_width, (r + 1) * block_width)
        volt_real = source_real_ref[rows, :] - drop_real
        volt_imag = source_imag_ref[rows, :] - drop_imag
        if last:
            outs[0][rows, :] = volt_real
            outs[1][rows, :] = volt_imag
            magnitude = jnp.sqrt(volt_real * volt_real + volt_imag * volt_imag)
            total = None
            for piece in split3(magnitude):
                term = lax.dot_general(pick, piece, (((1,), (1,)), ((), ())), preferred_element_type=f32)
                total = term if total is None else total + term
            for copy in range(outs[2].shape[0]):
                outs[2][copy, :, rows] = total
        else:
            current_real, current_imag = currents_of(volt_real, volt_imag, load_real_ref[rows, :], load_reactive_ref[rows, :])
            if size == GMAX:
                for copy in range(GMAX):
                    outs[0][copy, rows, :LANES] = current_real
                    outs[0][copy, rows, LANES:] = current_imag
            else:
                outs[0][rows, :LANES] = current_real
                outs[0][rows, LANES:] = current_imag


def sweep(place, column_blocks, impedance_real, impedance_imag, loads, windows, size, last, scen_count):
    phase_count, columns = loads[0].shape
    block_count, _, block_width, _ = impedance_real.shape
    smem, vmem = pl.BlockSpec(memory_space=pltpu.SMEM), pl.BlockSpec(memory_space=pltpu.VMEM)
    if last:
        shapes = [jax.ShapeDtypeStruct((phase_count, columns), f32)] * 2 + [jax.ShapeDtypeStruct((scen_count, TIMES, phase_count), f32)]
    else:
        shapes = [jax.ShapeDtypeStruct(((GMAX,) if size == GMAX else ()) + (phase_count, 2 * columns), bf16)]
    scratch = [] if len(windows) == 1 else [pltpu.VMEM((len(windows) * block_count, block_width, 2 * columns), bf16)]
    if size == GMAX or size == 1:
        windows = [windows[0].reshape(size * block_count, block_width, 2 * columns)]
    return pl.pallas_call(
        functools.partial(sweep_kernel, size=size, last=last),
        out_shape=shapes,
        in_specs=[smem, smem] + [vmem] * (6 + len(windows)),
        out_specs=[vmem] * len(shapes),
        scratch_shapes=scratch,
        compiler_params=pltpu.CompilerParams(vmem_limit_bytes=VMEM_BYTES),
        name="sweep",
    )(place, column_blocks, impedance_real, impedance_imag, *loads, *windows)


def branch_of(size, offset, net_count, scen_count):
    starts = range(offset, net_count - size + 1, size)
    rings = [[(s + a, s + (a + turn) % size) for s in starts for a in range(size)] for turn in range(1, size)]
    quads = [[(s + offset + a) % net_count for a in range(GMAX)] for s in range(0, net_count, GMAX)]

    def exchange(current):
        if size == GMAX:
            return [lax.all_to_all(current, "net", 0, 0, axis_index_groups=quads)]
        return [current] + [lax.ppermute(current, "net", pairs) for pairs in rings]

    def run(current, place, column_blocks, impedance_real, impedance_imag, loads):
        if size < GMAX:
            current = current[0]
        for turn in range(ITERS):
            made = sweep(place, column_blocks, impedance_real, impedance_imag, loads, exchange(current), size, turn == ITERS - 1, scen_count)
            current = made[0]
        return tuple(made)

    return run


def finish_kernel(sums_ref, out_ref, *, scen_total):
    total = sums_ref[0]
    for k in range(1, sums_ref.shape[0]):
        total = total + sums_ref[k]
    out_ref[...] = (100.0 * (1.0 - total / scen_total)).T


def shards(device_group, column_blocks, impedance_real, impedance_imag, building_phase, building_power, reactive_ratio, copula_normals, source_angle):
    net_count, scen_count = lax.axis_size("net"), lax.axis_size("scen")
    column_count = copula_normals.shape[1]
    scen_total = column_count // TIMES * scen_count
    where = jnp.stack([lax.axis_index("net"), lax.axis_index("scen")]).astype(jnp.int32)
    place, current, *loads = front(
        where, device_group, building_phase, building_power, reactive_ratio, copula_normals, source_angle, net_count, scen_total)
    kinds = [(1, 0)] + [(size, offset) for size in range(2, GMAX + 1) for offset in range(size)]
    volt_real, volt_imag, sums = lax.switch(
        place[0], [branch_of(size, offset, net_count, scen_count) for size, offset in kinds],
        current, place, column_blocks, impedance_real, impedance_imag, loads)
    sums = lax.all_to_all(sums, "scen", 0, 0)
    phase_count = volt_real.shape[0]
    drop_mean = pl.pallas_call(
        functools.partial(finish_kernel, scen_total=scen_total),
        out_shape=jax.ShapeDtypeStruct((phase_count, TIMES), f32),
        in_specs=[pl.BlockSpec(memory_space=pltpu.VMEM)],
        out_specs=pl.BlockSpec(memory_space=pltpu.VMEM),
        name="finish",
    )(sums)
    return volt_real, volt_imag, drop_mean


def solution(mesh):
    in_specs = (P(), P("net", None), P("net", None, None, None), P("net", None, None, None), P("net"), P("net"), P("net"), P("net", "scen"), P("net"))
    out_specs = (P("net", "scen"), P("net", "scen"), P("net", None))
    return jax.shard_map(shards, mesh=mesh, in_specs=in_specs, out_specs=out_specs, check_vma=False)
```

time: 171 us -> 102 us (0.60)
  the two profiles are of different devices: /device:TPU:224 before, /device:TPU:258 now
where the time goes in v1:
time: 102 us; the launch traced here: 101 us
  blocking collectives  81.9 us (80%)
  Pallas kernels  11.9 us (12%)
  local copies, waits for them, and re-layouts  6.12 us (6%)
    all_to_all x3, blocking collectives, exchange(): return [lax.all_to_all(current, 'net', 0, 0, axis_index_groups=quads)]  70.1 us
    all_to_all x1, blocking collectives, shards(): sums = lax.all_to_all(sums, 'scen', 0, 0)  11.9 us
    pallas_call x3, Pallas kernels, sweep(): pl.pallas_call(functools.partial(sweep_kernel, size=size, last=last), out...  8.02 us
    unnamed x13, local copies, waits for them, and re-layouts  6.1 us
    pallas_call x1, Pallas kernels, front(): pl.pallas_call(functools.partial(front_kernel, net_count=net_count, scen_...  2.08 us

profile of v1, /device:TPU:258, one launch (start us, length us, event | category | flops | bytes accessed | tf_op | source)
XLA Modules:
  0.0 101.3 jit_solution(94493887783363291)
XLA Ops:
  0.6 0.1 pad_add_fusion.where
  0.7 0.0 copy-start
  0.7 1.0 %copy-done = f32[1024,128]{1,0:T(8,128)S(1)} copy-done((f32[1024,128]{1,0:T(8,128)S(1)}, f32[1024,128]{1,0:T(8,128)}, u32[]{:S(2)}) %copy-start) | copy-done | bytes 524312
  1.8 0.0 copy-start.1
  1.8 0.7 copy-done.1
  2.4 0.0 copy-start.2
  2.4 0.7 copy-done.2
  3.1 0.0 copy-start.3
  3.1 0.7 copy-done.3
  3.8 0.0 copy-start.4
  3.8 0.7 copy-done.4
  4.5 0.0 copy-start.5
  4.5 0.7 copy-done.5
  5.2 2.1 %front.1 = (s32[4]{0:T(128)S(1)}, bf16[4,512,256]{2,1,0:T(8,128)(2,1)S(1)}, f32[512,128]{1,0:T(8,128)S(1)}, f32[512,128]{1,0:T(8,128)S(1)}, f32[512,128]{1,0:T(8,128)S(1)}, /*index=5*/f32[512,128]{1,0:T(8,128)S(1)}) custom-call(s32[2]{0:T(128)S(1)} %pad_add_fusion.where, s32[64]{0:T(128)S(1)} %copy-done.5, s32[8,128]{1,0:T(8,128)S(1)} %bitcast.48, ...), custom_call_target="tpu_custom_call" | custom-call | tf_op jit(solution)/shard_map/front/pallas_call | solution.py:91
  7.3 78.7 %conditional.1 = ((f32[512,128]{1,0:T(8,128)}, f32[512,128]{1,0:T(8,128)}, f32[8,16,512]{2,1,0:T(8,128)S(1)})) conditional(s32[]{:T(128)} %bitcast.26, (bf16[4,512,256]{2,1,0:T(8,128)(2,1)S(1)}, s32[4]{0:T(128)S(1)}, s32[4,12]{1,0:T(4,128)}, bf16[4,12,128,128]{3,2,1,0:T(8,128)(2,1)}, ...), branch_computations={%region_0.0_spmd, %region_1.0_spmd, %region_2.0_spmd, %region_3.0_... | conditional | bytes 19399756 | solution.py:216
  7.8 0.0 copy-start.15
  7.8 0.0 copy-start.35
  7.8 24.3 %all_to_all.62 = bf16[4,512,256]{2,1,0:T(8,128)(2,1)S(1)} all-to-all(bf16[4,512,256]{2,1,0:T(8,128)(2,1)S(1)} %get-tuple-element.269), channel_id=1, replica_groups={{24,32,40,48},{56,64,72,80},{88,96,104,112},{120,128,136,144},{152,160,..., dimensions={0} | all-to-all | bytes 2097152 | tf_op jit(solution)/shard_map/cond/branch_9_fun/all_to_all | solution.py:187
  32.1 0.0 copy-done.15
  32.1 0.0 copy-done.35
  32.1 2.5 %sweep.57 = bf16[4,512,256]{2,1,0:T(8,128)(2,1)S(1)} custom-call(s32[4]{0:T(128)S(1)} %get-tuple-element.261.place_ref, s32[4,12]{1,0:T(4,128)S(1)} %copy-done.35, bf16[4,12,128,128]{3,2,1,0:T(8,128)(2,1)S(1)} %copy-done.15, bf16[4,12,128,128]{3,2,1,0:T(8,128)(2,1)} %get-tuple-element.264.impedance_imag_ref, ...), custom_call_target="tpu_custom_call" | custom-call | tf_op jit(solution)/shard_map/cond/branch_9_fun/sweep/pallas_call | solution.py:169
  34.7 0.0 copy-start.25
  34.7 23.4 %all_to_all.63 = bf16[4,512,256]{2,1,0:T(8,128)(2,1)S(1)} all-to-all(bf16[4,512,256]{2,1,0:T(8,128)(2,1)S(1)} %sweep.57), channel_id=1, replica_groups={{24,32,40,48},{56,64,72,80},{88,96,104,112},{120,128,136,144},{152,160,..., dimensions={0} | all-to-all | bytes 2097152 | tf_op jit(solution)/shard_map/cond/branch_9_fun/all_to_all | solution.py:187
  58.1 0.0 copy-done.25
  58.1 1.7 %sweep.58 = bf16[4,512,256]{2,1,0:T(8,128)(2,1)S(1)} custom-call(s32[4]{0:T(128)S(1)} %get-tuple-element.261.place_ref, s32[4,12]{1,0:T(4,128)S(1)} %copy-done.35, bf16[4,12,128,128]{3,2,1,0:T(8,128)(2,1)S(1)} %copy-done.15, bf16[4,12,128,128]{3,2,1,0:T(8,128)(2,1)S(1)} %copy-done.25, f32[512,128]{1,0:T(8,128)S(1)} %get-tuple-element.265.load_real_ref, ...), custom_call_target="tpu_custom_call" | custom-call | tf_op jit(solution)/shard_map/cond/branch_9_fun/sweep/pallas_call | solution.py:169
  59.8 22.3 %all_to_all.64 = bf16[4,512,256]{2,1,0:T(8,128)(2,1)S(1)} all-to-all(bf16[4,512,256]{2,1,0:T(8,128)(2,1)S(1)} %sweep.58), channel_id=1, replica_groups={{24,32,40,48},{56,64,72,80},{88,96,104,112},{120,128,136,144},{152,160,..., dimensions={0} | all-to-all | bytes 2097152 | tf_op jit(solution)/shard_map/cond/branch_9_fun/all_to_all | solution.py:187
  82.1 3.8 %sweep.59 = (f32[512,128]{1,0:T(8,128)}, f32[512,128]{1,0:T(8,128)}, f32[8,16,512]{2,1,0:T(8,128)S(1)}) custom-call(s32[4]{0:T(128)S(1)} %get-tuple-element.261.place_ref, s32[4,12]{1,0:T(4,128)S(1)} %copy-done.35, bf16[4,12,128,128]{3,2,1,0:T(8,128)(2,1)S(1)} %copy-done.15, bf16[4,12,128,128]{3,2,1,0:T(8,128)(2,1)S(1)} %copy-done.25, ...), custom_call_target="tpu_custom_call" | custom-call | tf_op jit(solution)/shard_map/cond/branch_9_fun/sweep/pallas_call | solution.py:169
  85.9 11.9 %all_to_all.65.sums_ref = f32[8,16,512]{2,1,0:T(8,128)} all-to-all(f32[8,16,512]{2,1,0:T(8,128)S(1)} %get-tuple-element.290), channel_id=1, replica_groups=mesh['net'=64,'scen'=8] {'scen'}, dimensions={0} | all-to-all | bytes 524288 | tf_op jit(solution)/shard_map/all_to_all | solution.py:219
  97.8 1.8 %finish.1 = f32[512,16]{1,0:T(8,128)} custom-call(f32[8,16,512]{2,1,0:T(8,128)} %all_to_all.65.sums_ref), custom_call_target="tpu_custom_call" | custom-call | tf_op jit(solution)/shard_map/finish/pallas_call | solution.py:221
  99.7 1.7 %copy.12 = f32[512,16]{0,1:T(8,128)} copy(f32[512,16]{1,0:T(8,128)} %finish.1) | data formatting | bytes 65536
Async XLA Ops:
  0.7 1.0 %copy-start = (f32[1024,128]{1,0:T(8,128)S(1)}, f32[1024,128]{1,0:T(8,128)}, u32[]{:S(2)}) copy-start(f32[1024,128]{1,0:T(8,128)} %normals_ref.1) | copy-start | bytes 1572868
  1.8 0.7 copy-start.1
  2.4 0.7 copy-start.2
  3.1 0.7 copy-start.3
  3.8 0.7 copy-start.4
  4.5 0.7 copy-start.5
  7.8 24.3 %copy-start.15 = (bf16[4,12,128,128]{3,2,1,0:T(8,128)(2,1)S(1)}, bf16[4,12,128,128]{3,2,1,0:T(8,128)(2,1)}, u32[]{:S(2)}) copy-start(bf16[4,12,128,128]{3,2,1,0:T(8,128)(2,1)} %get-tuple-element.263.impedance_real_ref) | copy-start | bytes 4718596 | tf_op jit(solution)/shard_map/cond
  7.8 24.3 %copy-start.35 = (s32[4,12]{1,0:T(4,128)S(1)}, s32[4,12]{1,0:T(4,128)}, u32[]{:S(2)}) copy-start(s32[4,12]{1,0:T(4,128)} %get-tuple-element.262.column_ref) | copy-start | bytes 580 | tf_op jit(solution)/shard_map/cond
  34.7 23.4 %copy-start.25 = (bf16[4,12,128,128]{3,2,1,0:T(8,128)(2,1)S(1)}, bf16[4,12,128,128]{3,2,1,0:T(8,128)(2,1)}, u32[]{:S(2)}) copy-start(bf16[4,12,128,128]{3,2,1,0:T(8,128)(2,1)} %get-tuple-element.264.impedance_imag_ref) | copy-start | bytes 4718596 | tf_op jit(solution)/shard_map/cond

commit v2 on v1

v2 whole, which is shorter than its diff:
```python
import functools

import jax
import jax.numpy as jnp
from jax import lax
from jax.experimental import pallas as pl
from jax.experimental.pallas import tpu as pltpu
from jax.sharding import PartitionSpec as P

GMAX = 4
ITERS = 3
TIMES = 16
FLOOR = 0.49
LANES = 128
VMEM_BYTES = 14 * 1024 * 1024
f32, bf16 = jnp.float32, jnp.bfloat16


def split3(value):
    high = value.astype(bf16)
    rest = value - high.astype(f32)
    middle = rest.astype(bf16)
    return high, middle, (rest - middle.astype(f32)).astype(bf16)


def currents_of(volt_real, volt_imag, load_real, load_reactive):
    inverse = 1.0 / jnp.maximum(volt_real * volt_real + volt_imag * volt_imag, FLOOR)
    current_real = (load_real * volt_real + load_reactive * volt_imag) * inverse
    current_imag = (load_real * volt_imag - load_reactive * volt_real) * inverse
    return current_real.astype(bf16), current_imag.astype(bf16)


def front_kernel(group_any, column_any, phase_any, power_any, ratio_any, normals_any, angle_any,
                 place_ref, current_ref, load_real_ref, load_reactive_ref, columns_ref,
                 group_ref, column_ref, phase_ref, power_ref, ratio_ref, normals_ref, angle_ref, sems, normal_sems, *, scen_total):
    pairs = [(angle_any, angle_ref), (power_any, power_ref), (ratio_any, ratio_ref), (phase_any, phase_ref), (group_any, group_ref), (column_any, column_ref)]
    copies = [pltpu.make_async_copy(source, target, sems.at[k]) for k, (source, target) in enumerate(pairs)]
    blocks = phase_ref.shape[0]
    chunks = [pltpu.make_async_copy(normals_any.at[pl.ds(k * LANES, LANES)], normals_ref.at[pl.ds(k * LANES, LANES)], normal_sems.at[k]) for k in range(blocks)]
    for copy in copies + chunks:
        copy.start()
    net_index, scen_index = lax.axis_index("net"), lax.axis_index("scen")
    for copy in copies + chunks:
        copy.wait()
    angle = angle_ref[...]
    count = angle.shape[0]
    phase_count = count * LANES
    stacked = jnp.concatenate(
        [jnp.cos(angle), jnp.sin(angle), power_ref[...], ratio_ref[...], jnp.zeros((LANES - 2 * blocks - 2 * count, LANES), f32)], axis=0)
    columns = stacked.T
    columns_ref[...] = columns

    def column(k):
        return jnp.broadcast_to(columns[:, k:k + 1], (LANES, LANES))

    lane = lax.broadcasted_iota(jnp.int32, (1, LANES), 1)
    scenario = (scen_index * (LANES // TIMES) + lane // TIMES).astype(f32)
    level = 0.5 + scenario / (scen_total - 1)
    row = lax.broadcasted_iota(jnp.int32, (phase_count, LANES), 0) + net_index * phase_count
    hot = jnp.concatenate([jnp.where(row == phase_ref[k:k + 1, :], 1.0, 0.0).astype(bf16) for k in range(blocks)], axis=1)

    own = group_ref[net_index]
    before = jnp.int32(0)
    for distance in range(1, GMAX):
        other = group_ref[jnp.maximum(net_index - distance, 0)]
        before += ((net_index >= distance) & (other == own)).astype(jnp.int32)
    start = net_index - before
    size = own - start + 1
    block_count, slot_count = column_ref.shape
    place_ref[0] = jnp.where(size == 1, 0, jnp.where(size == 2, 1 + start % 2, jnp.where(size == 3, 3 + start % 3, 6 + start % 4)))
    for r in range(block_count):
        for s in range(slot_count):
            member = column_ref[r, s] - start * block_count
            device = member // block_count
            away = before - device
            away = jnp.where(away < 0, away + size, away)
            device = jnp.where(size < GMAX, away, device)
            place_ref[1 + r * slot_count + s] = device * block_count + member % block_count

    pieces = []
    for k in range(blocks):
        part = normals_ref[k * LANES:(k + 1) * LANES, :]
        real_power = column(2 * count + k) * level * jnp.exp(0.4 * part - 0.08)
        pieces.append(split3(jnp.concatenate([real_power, real_power * column(2 * count + blocks + k)], axis=1)))
    loads = None
    for piece in zip(*pieces):
        term = jnp.dot(hot, jnp.concatenate(piece, axis=0), preferred_element_type=f32)
        loads = term if loads is None else loads + term
    load_real_ref[...] = loads[:, :LANES]
    load_reactive_ref[...] = loads[:, LANES:]
    for k in range(count):
        rows = slice(k * LANES, (k + 1) * LANES)
        source_real = column(k)
        source_imag = column(count + k)
        current_real, current_imag = currents_of(source_real, source_imag, loads[rows, :LANES], loads[rows, LANES:])
        for copy in range(GMAX):
            current_ref[copy, rows, :LANES] = current_real
            current_ref[copy, rows, LANES:] = current_imag


def front(group, column_blocks, phase, power, ratio, normals, angle, scen_total):
    building_count, columns = normals.shape
    phase_count = angle.shape[0]
    smem, vmem = pl.BlockSpec(memory_space=pltpu.SMEM), pl.BlockSpec(memory_space=pltpu.VMEM)
    packed = [x.reshape(-1, LANES) for x in (phase, power, ratio)]
    angle = angle.reshape(-1, LANES)
    return pl.pallas_call(
        functools.partial(front_kernel, scen_total=scen_total),
        out_shape=[jax.ShapeDtypeStruct((1 + column_blocks.size,), jnp.int32), jax.ShapeDtypeStruct((GMAX, phase_count, 2 * columns), bf16)]
        + [jax.ShapeDtypeStruct((phase_count, columns), f32)] * 2 + [jax.ShapeDtypeStruct((LANES, LANES), f32)],
        in_specs=[pl.BlockSpec(memory_space=pltpu.HBM)] * 7,
        out_specs=[smem] + [vmem] * 4,
        scratch_shapes=[pltpu.SMEM(group.shape, jnp.int32), pltpu.SMEM(column_blocks.shape, jnp.int32)]
        + [pltpu.VMEM(x.shape, x.dtype) for x in (*packed, normals, angle)]
        + [pltpu.SemaphoreType.DMA((6,)), pltpu.SemaphoreType.DMA((building_count // LANES,))],
        compiler_params=pltpu.CompilerParams(vmem_limit_bytes=VMEM_BYTES),
        name="front",
    )(*[pltpu.with_memory_space_constraint(x, pltpu.HBM) for x in (group, column_blocks, *packed, normals, angle)])


def sweep_kernel(place_ref, impedance_real_ref, impedance_imag_ref, load_real_ref, load_reactive_ref, columns_ref, *refs, size, last):
    parts = 1 if size == GMAX else size
    window_refs, refs = refs[:parts], list(refs[parts:])
    block_count, slot_count, block_width, _ = impedance_real_ref.shape
    live = min(slot_count, size * block_count)
    window_ref = window_refs[0]
    if parts > 1:
        window_ref = refs.pop()
        for k in range(parts):
            window_ref[k * block_count:(k + 1) * block_count] = window_refs[k][...].reshape(block_count, block_width, -1)
    copies = []
    for r in range(block_count):
        left_real, left_imag, right = [], [], []
        for s in range(live):
            left_real.append(impedance_real_ref[r, s])
            left_imag.append(impedance_imag_ref[r, s])
            right.append(window_ref[place_ref[1 + r * slot_count + s]])
        left = jnp.concatenate([jnp.concatenate(left_real, axis=1), jnp.concatenate(left_imag, axis=1)], axis=0)
        product = jnp.dot(left, jnp.concatenate(right, axis=0), preferred_element_type=f32)
        drop_real = product[:block_width, :LANES] - product[block_width:, LANES:]
        drop_imag = product[:block_width, LANES:] + product[block_width:, :LANES]
        rows = slice(r * block_width, (r + 1) * block_width)
        volt_real = jnp.broadcast_to(columns_ref[:, r:r + 1], (block_width, LANES)) - drop_real
        volt_imag = jnp.broadcast_to(columns_ref[:, block_count + r:block_count + r + 1], (block_width, LANES)) - drop_imag
        if last:
            volt_real_any, volt_imag_any, sums_ref, volt_ref, sems = refs
            volt_ref[0, rows, :] = volt_real
            volt_ref[1, rows, :] = volt_imag
            for k, target in enumerate((volt_real_any, volt_imag_any)):
                span = pl.ds(r * block_width, block_width)
                copies.append(pltpu.make_async_copy(volt_ref.at[k, span], target.at[span], sems.at[k, r]))
                copies[-1].start()
            turned = jnp.sqrt(volt_real * volt_real + volt_imag * volt_imag).T
            total = turned[:TIMES]
            for s in range(1, LANES // TIMES):
                total = total + turned[s * TIMES:(s + 1) * TIMES]
            for copy in range(sums_ref.shape[0]):
                sums_ref[copy, :, rows] = total
        else:
            current_real, current_imag = currents_of(volt_real, volt_imag, load_real_ref[rows, :], load_reactive_ref[rows, :])
            for copy in range(GMAX if size == GMAX else 1):
                refs[0][copy, rows, :LANES] = current_real
                refs[0][copy, rows, LANES:] = current_imag
    for copy in copies:
        copy.wait()


def sweep(place, impedance_real, impedance_imag, loads, windows, size, last, scen_count):
    phase_count, columns = loads[0].shape
    block_count, _, block_width, _ = impedance_real.shape
    smem, vmem = pl.BlockSpec(memory_space=pltpu.SMEM), pl.BlockSpec(memory_space=pltpu.VMEM)
    scratch = []
    if last:
        shapes = [jax.ShapeDtypeStruct((phase_count, columns), f32)] * 2 + [jax.ShapeDtypeStruct((scen_count, TIMES, phase_count), f32)]
        out_specs = [pl.BlockSpec(memory_space=pltpu.HBM)] * 2 + [vmem]
        scratch = [pltpu.VMEM((2, phase_count, columns), f32), pltpu.SemaphoreType.DMA((2, block_count))]
    else:
        shapes = [jax.ShapeDtypeStruct((GMAX if size == GMAX else 1, phase_count, 2 * columns), bf16)]
        out_specs = [vmem]
    if len(windows) > 1:
        scratch.append(pltpu.VMEM((len(windows) * block_count, block_width, 2 * columns), bf16))
    else:
        windows = [windows[0].reshape(size * block_count, block_width, 2 * columns)]
    return pl.pallas_call(
        functools.partial(sweep_kernel, size=size, last=last),
        out_shape=shapes,
        in_specs=[smem] + [vmem] * (5 + len(windows)),
        out_specs=out_specs,
        scratch_shapes=scratch,
        compiler_params=pltpu.CompilerParams(vmem_limit_bytes=VMEM_BYTES),
        name="sweep",
    )(place, impedance_real, impedance_imag, *loads, *windows)


def branch_of(size, offset, net_count, scen_count):
    starts = range(offset, net_count - size + 1, size)
    rings = [[(s + a, s + (a + turn) % size) for s in starts for a in range(size)] for turn in range(1, size)]
    quads = [[(s + offset + a) % net_count for a in range(GMAX)] for s in range(0, net_count, GMAX)]

    def exchange(current):
        if size == GMAX:
            return [lax.all_to_all(current, "net", 0, 0, axis_index_groups=quads)]
        return [current] + [lax.ppermute(current, "net", pairs) for pairs in rings]

    def run(current, place, impedance_real, impedance_imag, loads):
        if size < GMAX:
            current = current[:1]
        for turn in range(ITERS):
            made = sweep(place, impedance_real, impedance_imag, loads, exchange(current), size, turn == ITERS - 1, scen_count)
            current = made[0]
        return tuple(made)

    return run


def shards(device_group, column_blocks, impedance_real, impedance_imag, building_phase, building_power, reactive_ratio, copula_normals, source_angle):
    net_count, scen_count = lax.axis_size("net"), lax.axis_size("scen")
    column_count = copula_normals.shape[1]
    scen_total = column_count // TIMES * scen_count
    place, current, *loads = front(
        device_group, column_blocks, building_phase, building_power, reactive_ratio, copula_normals, source_angle, scen_total)
    kinds = [(1, 0)] + [(size, offset) for size in range(2, GMAX + 1) for offset in range(size)]
    volt_real, volt_imag, sums = lax.switch(
        place[0], [branch_of(size, offset, net_count, scen_count) for size, offset in kinds],
        current, place, impedance_real, impedance_imag, loads)
    sums = lax.all_to_all(sums, "scen", 0, 0)
    drop_mean = 100.0 * (1.0 - jnp.sum(sums, axis=0) / scen_total)
    return volt_real, volt_imag, drop_mean.T


def solution(mesh):
    in_specs = (P(), P("net", None), P("net", None, None, None), P("net", None, None, None), P("net"), P("net"), P("net"), P("net", "scen"), P("net"))
    out_specs = (P("net", "scen"), P("net", "scen"), P("net", None))
    return jax.shard_map(shards, mesh=mesh, in_specs=in_specs, out_specs=out_specs, check_vma=False)
```

time: 102 us -> 90.9 us (0.89)
  the two profiles are of different devices: /device:TPU:258 before, /device:TPU:98 now
where the time goes in v2:
time: 90.9 us; the launch traced here: 90.6 us
  blocking collectives  78.2 us (86%)
  Pallas kernels  10.2 us (11%)
    all_to_all x3, blocking collectives, exchange(): return [lax.all_to_all(current, 'net', 0, 0, axis_index_groups=quads)]  66.4 us
    all_to_all x1, blocking collectives, shards(): sums = lax.all_to_all(sums, 'scen', 0, 0)  11.8 us
    pallas_call x3, Pallas kernels, sweep(): pl.pallas_call(functools.partial(sweep_kernel, size=size, last=last), out...  6.46 us
    pallas_call x1, Pallas kernels, front(): pl.pallas_call(functools.partial(front_kernel, scen_total=scen_total), ou...  3.69 us

profile of v2, /device:TPU:98, one launch (start us, length us, event | category | flops | bytes accessed | tf_op | source)
XLA Modules:
  0.0 90.6 jit_solution(4077187504706389254)
XLA Ops:
  0.6 3.7 %front.1 = (s32[49]{0:T(128)S(1)}, bf16[4,512,256]{2,1,0:T(8,128)(2,1)S(1)}, f32[512,128]{1,0:T(8,128)S(1)}, f32[512,128]{1,0:T(8,128)S(1)}, f32[128,128]{1,0:T(8,128)S(1)}) custom-call(s32[64]{0:T(128)} %group_any.1, s32[4,12]{1,0:T(4,128)} %column_any.1, s32[8,128]{1,0:T(8,128)} %bitcast.39, f32[8,128]{1,0:T(8,128)} %bitcast.40, f32[8,128]{1,0:T(8,128)} %bitcast.41, ...), custom_call_target="tpu_custom_call" | custom-call | tf_op jit(solution)/shard_map/front/pallas_call | solution.py:107
  4.4 73.8 %conditional.1 = ((f32[512,128]{1,0:T(8,128)}, f32[512,128]{1,0:T(8,128)}, f32[8,16,512]{2,1,0:T(8,128)S(1)})) conditional(s32[]{:T(128)} %bitcast.19, (bf16[4,512,256]{2,1,0:T(8,128)(2,1)S(1)}, s32[49]{0:T(128)S(1)}, bf16[4,12,128,128]{3,2,1,0:T(8,128)(2,1)}, bf16[4,12,128,128]{3,2,1,0:T(8,128)(2,1)}, ...), branch_computations={%region_0.0_spmd, %region_1.0_spmd, %region_2.0_spmd, %region_3.0_... | conditional | bytes 19398960 | solution.py:223
  4.9 0.0 copy-start.9
  4.9 23.1 %all_to_all.62 = bf16[4,512,256]{2,1,0:T(8,128)(2,1)S(1)} all-to-all(bf16[4,512,256]{2,1,0:T(8,128)(2,1)S(1)} %get-tuple-element.209), channel_id=1, replica_groups={{24,32,40,48},{56,64,72,80},{88,96,104,112},{120,128,136,144},{152,160,..., dimensions={0} | all-to-all | bytes 2097152 | tf_op jit(solution)/shard_map/cond/branch_9_fun/all_to_all | solution.py:202
  28.0 0.0 copy-done.9
  28.0 2.5 %sweep.57 = bf16[4,512,256]{2,1,0:T(8,128)(2,1)S(1)} custom-call(s32[49]{0:T(128)S(1)} %get-tuple-element.203.place_ref, bf16[4,12,128,128]{3,2,1,0:T(8,128)(2,1)S(1)} %copy-done.9, bf16[4,12,128,128]{3,2,1,0:T(8,128)(2,1)} %get-tuple-element.205.impedance_imag_ref, f32[512,128]{1,0:T(8,128)S(1)} %get-tuple-element.206.load_real_ref, ...), custom_call_target="tpu_custom_call" | custom-call | tf_op jit(solution)/shard_map/cond/branch_9_fun/sweep/pallas_call | solution.py:184
  30.5 0.0 copy-start.19
  30.5 22.2 %all_to_all.63 = bf16[4,512,256]{2,1,0:T(8,128)(2,1)S(1)} all-to-all(bf16[4,512,256]{2,1,0:T(8,128)(2,1)S(1)} %sweep.57), channel_id=1, replica_groups={{24,32,40,48},{56,64,72,80},{88,96,104,112},{120,128,136,144},{152,160,..., dimensions={0} | all-to-all | bytes 2097152 | tf_op jit(solution)/shard_map/cond/branch_9_fun/all_to_all | solution.py:202
  52.7 0.0 copy-done.19
  52.7 1.6 %sweep.58 = bf16[4,512,256]{2,1,0:T(8,128)(2,1)S(1)} custom-call(s32[49]{0:T(128)S(1)} %get-tuple-element.203.place_ref, bf16[4,12,128,128]{3,2,1,0:T(8,128)(2,1)S(1)} %copy-done.9, bf16[4,12,128,128]{3,2,1,0:T(8,128)(2,1)S(1)} %copy-done.19, f32[512,128]{1,0:T(8,128)S(1)} %get-tuple-element.206.load_real_ref, ...), custom_call_target="tpu_custom_call" | custom-call | tf_op jit(solution)/shard_map/cond/branch_9_fun/sweep/pallas_call | solution.py:184
  54.4 21.1 %all_to_all.64 = bf16[4,512,256]{2,1,0:T(8,128)(2,1)S(1)} all-to-all(bf16[4,512,256]{2,1,0:T(8,128)(2,1)S(1)} %sweep.58), channel_id=1, replica_groups={{24,32,40,48},{56,64,72,80},{88,96,104,112},{120,128,136,144},{152,160,..., dimensions={0} | all-to-all | bytes 2097152 | tf_op jit(solution)/shard_map/cond/branch_9_fun/all_to_all | solution.py:202
  75.5 2.4 %sweep.59 = (f32[512,128]{1,0:T(8,128)}, f32[512,128]{1,0:T(8,128)}, f32[8,16,512]{2,1,0:T(8,128)S(1)}) custom-call(s32[49]{0:T(128)S(1)} %get-tuple-element.203.place_ref, bf16[4,12,128,128]{3,2,1,0:T(8,128)(2,1)S(1)} %copy-done.9, bf16[4,12,128,128]{3,2,1,0:T(8,128)(2,1)S(1)} %copy-done.19, f32[512,128]{1,0:T(8,128)S(1)} %get-tuple-element.206.load_real_ref, ...), custom_call_target="tpu_custom_call" | custom-call | tf_op jit(solution)/shard_map/cond/branch_9_fun/sweep/pallas_call | solution.py:184
  78.1 11.8 %all_to_all.65 = f32[8,16,512]{2,1,0:T(8,128)S(1)} all-to-all(f32[8,16,512]{2,1,0:T(8,128)S(1)} %get-tuple-element.228), channel_id=1, replica_groups=mesh['net'=64,'scen'=8] {'scen'}, dimensions={0} | all-to-all | bytes 524288 | tf_op jit(solution)/shard_map/all_to_all | solution.py:226
  90.0 0.6 multiply_bitcast_fusion
  (1 shorter events, 0.0 us)
Async XLA Ops:
  4.9 23.1 %copy-start.9 = (bf16[4,12,128,128]{3,2,1,0:T(8,128)(2,1)S(1)}, bf16[4,12,128,128]{3,2,1,0:T(8,128)(2,1)}, u32[]{:S(2)}) copy-start(bf16[4,12,128,128]{3,2,1,0:T(8,128)(2,1)} %get-tuple-element.204.impedance_real_ref) | copy-start | bytes 4718596 | tf_op jit(solution)/shard_map/cond
  30.5 22.2 %copy-start.19 = (bf16[4,12,128,128]{3,2,1,0:T(8,128)(2,1)S(1)}, bf16[4,12,128,128]{3,2,1,0:T(8,128)(2,1)}, u32[]{:S(2)}) copy-start(bf16[4,12,128,128]{3,2,1,0:T(8,128)(2,1)} %get-tuple-element.205.impedance_imag_ref) | copy-start | bytes 4718596 | tf_op jit(solution)/shard_map/cond
